TPU v7x, 32 devices: a whole 2x2x4 slice. The times are simulated.
32 devices in a mesh: leaf: 16 (over z, y, core), list: 2 (over x).
Axes of the slice: x: 2, y: 2, z: 4, core: 2. Of those that a mesh axis runs over, the one named last changes fastest.
Arguments:
- points: bfloat16 [32, 65536], P(None, 'leaf')
- charges: bfloat16 [32, 65536], P(None, 'leaf'), may hold values from -0.59765625 to 0.59765625
- leaf_ids: int32 [256, 128], P('leaf'), may hold values from 0 to 255, as said below
- inner_ids: int32 [240, 128], P('leaf'), may hold values from 0 to 255, as said below
- upper_ids_first: int32 [8, 128], replicated, may hold values from 0 to 255, as said below
- upper_ids_second: int32 [4, 128], replicated, may hold values from 0 to 255, as said below
- upper_ids_third: int32 [2, 128], replicated, may hold values from 0 to 255, as said below
- leaf_maps: bfloat16 [256, 128, 256], P('leaf'), may hold values from -0.375 to 0.375
- inner_maps: bfloat16 [240, 128, 256], P('leaf'), may hold values from -0.4375 to 0.4375
- upper_maps_first: bfloat16 [1024, 256], P('leaf'), may hold values from -0.4375 to 0.4375
- upper_maps_second: bfloat16 [512, 256], P('leaf'), may hold values from -0.4375 to 0.4375
- upper_maps_third: bfloat16 [256, 256], P('leaf'), may hold values from -0.4375 to 0.4375
- near_lists: int32 [256, 32], P('leaf', 'list'), may hold values from -1 to 255, as said below
- far_inner: int32 [496, 32], P('leaf', 'list'), may hold values from 0 to 255, as said below
- far_upper_first: int32 [8, 32], P(None, 'list'), may hold values from 0 to 7
- far_upper_second: int32 [4, 32], P(None, 'list'), may hold values from 0 to 3
- far_upper_third: int32 [2, 32], P(None, 'list'), may hold values from 0 to 1
Outputs:
- potentials: float32 [32, 65536], P(None, ('leaf', 'list'))
Inputs may be any that keep to these rules, and one draw needn't show every extreme that they name: `leaf_ids`: each row holds 128 distinct columns of its leaf. `inner_ids`: each row holds 128 distinct columns of its node's 2 * 128 child skeleton columns. `upper_ids_first`: each row holds 128 distinct columns of its node's 2 * 128 child skeleton columns. `upper_ids_second`: each row holds 128 distinct columns of its node's 2 * 128 child skeleton columns. `upper_ids_third`: each row holds 128 distinct columns of its node's 2 * 128 child skeleton columns. `near_lists`: each row starts with one or more leaf numbers and is -1 after them; some row has 32 leaf numbers. A leaf number s in row i satisfies |s // 16 - i // 16| <= 1. `far_inner`: an entry s of node i at level l satisfies |s // (16 >> l) - i // (16 >> l)| <= 1, both numbered within level l.
All inputs are finite; a program needn't handle non-finite values.
Results may differ from a plain program's by a relative error of at most 0.01.
Values may be sent and summed in bfloat16 or wider, within the bound.
No kernel may reach another device: no remote copies, remote signals or barrier semaphores. Data moves between devices by JAX's collectives and lax.ppermute only.
A program may use at most 128 MiB of HBM per device.

v0:
```python
import functools
import math

import jax
import jax.numpy as jnp
from jax import lax
from jax.experimental import pallas as pl
from jax.experimental.pallas import tpu as pltpu
from jax.sharding import PartitionSpec as P

BF = jnp.bfloat16
F32 = jnp.float32
NORM_ROWS = 16
VMEM_BYTES = 40 * 2**20
UP_VMEM_BYTES = 60 * 2**20
LANES = 128
NEAR_UNIT = 1
FAR_UNIT = 2
NEAR_SIZES = (NEAR_UNIT, 16)
FAR_SIZES = (FAR_UNIT, 16)


def nt(a, b):
    return lax.dot_general(a, b, (((1,), (1,)), ((), ())), preferred_element_type=F32)


def nn(a, b):
    return jnp.dot(a, b, preferred_element_type=F32)


def pick(coords, ids):
    shape = (coords.shape[1], ids.shape[1])
    hot = (lax.broadcasted_iota(jnp.int32, shape, 0) == ids).astype(BF)
    return nn(coords, hot).astype(BF)


def norm_rows(coords, first):
    wide = coords.astype(F32)
    norm = jnp.sum(wide * wide, axis=0, keepdims=True)
    high = norm.astype(BF).astype(F32)
    rest = norm - high
    middle = rest.astype(BF).astype(F32)
    low = rest - middle
    row = lax.broadcasted_iota(jnp.int32, (NORM_ROWS, coords.shape[1]), 0)
    parts = jnp.where(row == first, high, jnp.where(row == first + 1, middle, low))
    inside = (row >= first) & (row < first + 3)
    ones = (row < 6) & jnp.logical_not(inside)
    return jnp.where(inside, parts, jnp.where(ones, 1.0, 0.0)).astype(BF)


def target_side(coords):
    rows = jnp.concatenate(
        [coords.astype(F32) * -2.0, norm_rows(coords, 0).astype(F32)], axis=0
    )
    depth, count = rows.shape
    padded = jnp.concatenate([rows, jnp.zeros((128 - depth, count), F32)], axis=0)
    return padded.T.astype(BF)[:, :depth]


def kernel_block(goal, source, scale):
    return jnp.exp2(nn(goal, source) * scale).astype(BF)


def halves(value):
    high = value.astype(BF)
    low = (value - high.astype(F32)).astype(BF)
    return jnp.concatenate([high, low], axis=0)


def through(value, matrix):
    count = value.shape[0]
    both = nn(halves(value), matrix)
    return both[:count] + both[count:]


def up_body(levels, *refs):
    sources, (bundle, blocks), held, sems = refs[:9], refs[9:11], refs[11:20], refs[20]
    copies = [pltpu.make_async_copy(src, dst, sems.at[i]) for i, (src, dst) in enumerate(zip(sources, held))]
    for copy in copies:
        copy.start()
    points, charges, leaf_ids, inner_ids, leaf_maps, inner_maps = held[:6]
    leaf_count, skel, leaf_size = leaf_maps.shape
    dim = points.shape[0]

    def put(node, place, load):
        cols = slice((node % 2) * skel, (node % 2 + 1) * skel)
        bundle[leaf_count + node // 2, :dim, cols] = place
        bundle[leaf_count + node // 2, dim:, cols] = load

    for i in (0, 2):
        copies[i].wait()
    places = []
    for i in range(leaf_count):
        mine = points[:, i * leaf_size : (i + 1) * leaf_size]
        bundle[i, :dim] = mine
        places.append(pick(mine, leaf_ids[i : i + 1]))
    for i in (1, 4):
        copies[i].wait()
    for i in range(leaf_count):
        mine = charges[:, i * leaf_size : (i + 1) * leaf_size]
        bundle[i, dim:] = mine
        put(i, places[i], nt(mine, leaf_maps[i]).astype(BF))
    for i in (3, 5):
        copies[i].wait()
    below, here, row = 0, leaf_count, 0
    for degree in range(1, levels + 1):
        for i in range(leaf_count >> degree):
            pair = bundle[leaf_count + below // 2 + i]
            put(here + i, pick(pair[:dim], inner_ids[row : row + 1]), nt(pair[dim:], inner_maps[row]).astype(BF))
            row += 1
        below = here
        here += leaf_count >> degree
    for node in range(here, 2 * leaf_count):
        empty = jnp.zeros((dim, skel), BF)
        put(node, empty, jnp.zeros((bundle.shape[1] - dim, skel), BF))
    last = here - 1
    root = bundle[leaf_count + last // 2, :, (last % 2) * skel : (last % 2 + 1) * skel]
    parts = [jnp.concatenate([root[:dim], root[dim:]], axis=1)]
    for i in (6, 7, 8):
        copies[i].wait()
        parts.append(held[i][...])
    whole = jnp.concatenate(parts, axis=0)
    for device in range(blocks.shape[0]):
        blocks[device] = whole


def ceil_to(value, unit):
    return -(-value // unit) * unit


class Plan:
    def __init__(self, leaf_count, share, levels, slots, upper_counts):
        self.leaf_count, self.share, self.levels, self.slots = leaf_count, share, levels, slots
        self.per_side = 2 * leaf_count - 1
        self.counts = [max(1, share >> degree) for degree in range(levels + 1)]
        self.first_rows = [2 * leaf_count - 2 * (leaf_count >> degree) for degree in range(levels + 1)]
        self.targets = sum(self.counts)
        self.far_row = share
        self.upper_row = share + self.targets
        self.rows = self.upper_row + len(upper_counts)
        self.upper_counts = upper_counts
        self.upper_bases = [sum(upper_counts[:i]) for i in range(len(upper_counts))]
        trees = [leaf_count >> degree for degree in range(levels + 1)]
        def room(count, unit):
            return ceil_to(min(slots, count), unit)

        most = [
            share * room(leaf_count, NEAR_UNIT),
            share * room(2 * leaf_count, NEAR_UNIT),
            sum(c * room(t, FAR_UNIT) for c, t in zip(self.counts, trees)),
            sum(c * room(2 * t, FAR_UNIT) for c, t in zip(self.counts, trees)),
            sum(room(c, FAR_UNIT) for c in upper_counts),
        ]
        self.starts, at = [], 0
        for count in most:
            self.starts.append(at)
            at += ceil_to(count, LANES)
        self.table_rows = at // LANES
        self.out_rows = ceil_to(self.table_rows + 1, 8)
        width = max(3 * leaf_count, 3 * self.per_side, sum(upper_counts))
        assert width <= LANES and self.rows <= LANES and slots <= LANES


def table_body(plan, n_chunks, spot, *refs):
    chunks, (out, held) = refs[:n_chunks], refs[n_chunks:]
    position, member = spot[0], spot[1]
    leaf_count, share = plan.leaf_count, plan.share
    held[...] = jnp.full(held.shape, -1, jnp.int32)

    def rows_of(start, count):
        return jnp.concatenate([chunk[pl.ds(start, count)] for chunk in chunks], axis=1)

    slots = plan.slots
    entries = rows_of(member * share, share)
    held[:share, :slots] = jnp.where(entries >= 0, entries - (position - 1) * leaf_count, -1)
    row = plan.far_row
    for degree in range(plan.levels + 1):
        count = plan.counts[degree]
        shift = plan.levels - degree
        entries = rows_of(leaf_count + plan.first_rows[degree] + ((member * share) >> degree), count)
        side = (entries >> shift) - position + 1
        within = entries & ((1 << shift) - 1)
        held[row : row + count, :slots] = side * plan.per_side + plan.first_rows[degree] + within
        row += count
    at = leaf_count + plan.per_side
    for level, count in enumerate(plan.upper_counts):
        entries = rows_of(at + (position >> (level + 1)), 1)
        held[row : row + 1, :slots] = entries + plan.upper_bases[level]
        row += 1
        at += count

    across = held[...].astype(F32).T
    square = (LANES, LANES)
    down_i = lax.broadcasted_iota(jnp.int32, square, 0)
    across_i = lax.broadcasted_iota(jnp.int32, square, 1)
    source = down_i.astype(F32)
    often = jnp.zeros(square, F32)
    for k in range(slots):
        often += jnp.where(across[k : k + 1] == source, 1.0, 0.0)
    near_r, far_r = plan.far_row, plan.upper_row
    half = jnp.where(across_i < near_r, leaf_count, plan.per_side)
    inside = (down_i >= half) & (down_i < 2 * half)
    own = (inside & (across_i < far_r)) | ((across_i >= far_r) & (across_i < plan.rows))
    present = often > 0.0
    is_own = jnp.where(present & own, 1.0, 0.0)
    is_rim = jnp.where(present & jnp.logical_not(own), 1.0, 0.0)
    before = jnp.where(across_i < down_i, 1.0, 0.0).astype(BF)
    kind_down = (down_i >= near_r).astype(jnp.int32) + (down_i >= far_r).astype(jnp.int32)
    kind_across = (across_i >= near_r).astype(jnp.int32) + (across_i >= far_r).astype(jnp.int32)
    earlier = jnp.where((down_i < across_i) & (kind_down == kind_across), 1.0, 0.0).astype(BF)
    row_kind = kind_across[:1]
    lane = across_i[:1]
    totals = []
    rank = jnp.zeros(square, F32)
    for mask, starts in ((is_own, (0, 2, 4)), (is_rim, (1, 3, 4))):
        unit = jnp.where(row_kind == 0, float(NEAR_UNIT), float(FAR_UNIT))
        sums = jnp.sum(mask, axis=0, keepdims=True)
        sums = jnp.floor((sums + (unit - 1.0)) / unit) * unit
        base = nn(jnp.broadcast_to(sums, (16, LANES)).astype(BF), earlier)[:1]
        first = jnp.where(
            row_kind == 0,
            float(plan.starts[starts[0]]),
            jnp.where(row_kind == 1, float(plan.starts[starts[1]]), float(plan.starts[starts[2]])),
        )
        rank += mask * (nn(before, mask.astype(BF)) + base + first)
        for kind in range(3):
            totals.append(jnp.sum(jnp.where(row_kind == kind, sums, 0.0), axis=1, keepdims=True))
    spot_of = jnp.where(present & (across_i < plan.rows), rank, -1.0)
    spot_by_row = spot_of.T
    often_by_row = often.T
    part_rows = ceil_to(3 * plan.table_rows, 16)
    shape = (part_rows, LANES)
    part_i = lax.broadcasted_iota(jnp.int32, shape, 0)
    source_i = lax.broadcasted_iota(jnp.int32, shape, 1).astype(F32)
    part = (part_i >= plan.table_rows).astype(jnp.int32) + (part_i >= 2 * plan.table_rows).astype(jnp.int32)
    low = ((part_i - part * plan.table_rows) * LANES).astype(F32)
    slot_i = across_i.astype(F32)
    found = jnp.zeros(shape, F32)
    spot_low = spot_of - jnp.floor(spot_of * (1.0 / LANES)) * LANES
    spot_low = jnp.where(spot_of < 0.0, -1.0, spot_low)
    for r in range(plan.rows):
        where_to = spot_by_row[r : r + 1]
        value = jnp.where(part == 0, source_i, jnp.where(part == 1, often_by_row[r : r + 1], float(r)))
        value = jnp.where((where_to >= low) & (where_to < low + LANES), value, 0.0)
        hot = jnp.where(spot_low[:, r : r + 1] == slot_i, 1.0, 0.0).astype(BF)
        found += nn(value.astype(BF), hot)
    found = found.astype(jnp.int32)
    n = plan.table_rows
    out[:n] = found[:n] + found[n : 2 * n] * LANES + found[2 * n : 3 * n] * (LANES * 64)
    counts = jnp.zeros((1, LANES), F32)
    for at, total in enumerate((totals[0], totals[3], totals[1], totals[4], totals[2])):
        counts = jnp.where(lane == at, total, counts)
    out[n : n + 1] = counts.astype(jnp.int32)


def decode(table, at):
    code = table[at // LANES, at % LANES]
    return code & (LANES - 1), ((code >> 7) & 63).astype(F32), code >> 13


def add_items(plan, table, kind, sizes, goals, nodes, dim, scale, acc, first_row, source_base):
    unit, unroll = sizes
    depth = dim + NORM_ROWS
    start = plan.starts[kind]
    total = table[plan.table_rows, kind]
    group = unit * unroll

    def some(step, _):
        terms = []
        for k in range(unroll):
            items = [decode(table, start + step * group + k * unit + u) for u in range(unit)]
            sources = [jnp.maximum(item[0] - source_base(item[0]), 0) for item in items]
            row = jnp.maximum(items[0][2] - first_row, 0)
            places = jnp.concatenate([nodes[source, :depth] for source in sources], axis=1)
            block = jnp.exp2(nn(goals[row], places) * scale)
            if unit > 1:
                width = block.shape[1] // unit
                block = jnp.concatenate(
                    [block[:, u * width : (u + 1) * width] * items[u][1] for u in range(unit)], axis=1
                )
            loads = jnp.concatenate([nodes[source, depth:] for source in sources], axis=1)
            term = nt(loads, block.astype(BF))
            terms.append((row, term if unit > 1 else term * items[0][1]))
        for row, term in terms:
            acc[row] += term
        return 0

    lax.fori_loop(0, (total + group - 1) // group, some, 0)


def load_leaf(nodes, at, both, dim):
    nodes[at, :dim] = both[:dim]
    nodes[at, dim : dim + NORM_ROWS] = norm_rows(both[:dim], 3)
    nodes[at, dim + NORM_ROWS :] = both[dim:]


def load_side(plan, bundle, leaves, nodes, leaf_at, node_at, dim):
    skel = nodes.shape[2]
    for i in range(plan.leaf_count):
        load_leaf(leaves, leaf_at + i, bundle[i], dim)
    for i in range(plan.per_side):
        cols = slice((i % 2) * skel, (i % 2 + 1) * skel)
        load_leaf(nodes, node_at + i, bundle[plan.leaf_count + i // 2, :, cols], dim)


def own_body(plan, dim, scale, spot, table, bundle, near, far, near_goals, far_goals, leaves, nodes):
    member = spot[1]
    leaf_count, share = plan.leaf_count, plan.share
    load_side(plan, bundle, leaves, nodes, 0, 0, dim)
    for t in range(share):
        near_goals[t] = target_side(leaves[member * share + t, :dim])
    made = 0
    for degree in range(plan.levels + 1):
        start = plan.first_rows[degree] + ((member * share) >> degree)
        for t in range(plan.counts[degree]):
            far_goals[made + t] = target_side(nodes[start + t, :dim])
        made += plan.counts[degree]
    near[...] = jnp.zeros_like(near)
    far[...] = jnp.zeros_like(far)
    add_items(plan, table, 0, NEAR_SIZES, near_goals, leaves, dim, scale, near, 0, lambda s: leaf_count)
    add_items(plan, table, 2, FAR_SIZES, far_goals, nodes, dim, scale, far, plan.far_row, lambda s: plan.per_side)


def rim_body(plan, dim, scale, table, left, right, near_in, far_in, near_goals, far_goals, near, far, leaves, nodes):
    leaf_count, per_side = plan.leaf_count, plan.per_side
    load_side(plan, left, leaves, nodes, 0, 0, dim)
    load_side(plan, right, leaves, nodes, leaf_count, per_side, dim)
    near[...] = near_in[...]
    far[...] = far_in[...]

    def rim(count):
        return lambda s: jnp.where(s >= 2 * count, count, 0)

    add_items(plan, table, 1, NEAR_SIZES, near_goals, leaves, dim, scale, near, 0, rim(leaf_count))
    add_items(plan, table, 3, FAR_SIZES, far_goals, nodes, dim, scale, far, plan.far_row, rim(per_side))


def down_body(plan, dim, scale, spot, table, gathered, ids1, ids2, ids3, far, near, inner_maps, leaf_maps, out, nodes, goals, acc):
    leaf_count, skel, leaf_size = leaf_maps.shape
    share, levels = plan.share, plan.levels
    depth = dim + NORM_ROWS
    position, member = spot[0], spot[1]
    all_ids = (ids1, ids2, ids3)

    offsets = []
    offset = dim
    for level, n_nodes in enumerate(plan.upper_counts):
        group_size = 2 << level
        rows = skel // group_size
        base = plan.upper_bases[level]

        def one_node(j, _, level=level, base=base, offset=offset, group_size=group_size, rows=rows):
            if level == 0:
                left, right = gathered[2 * j, :dim], gathered[2 * j + 1, :dim]
                coords = jnp.concatenate([left[:, :skel], right[:, :skel]], axis=1)
                loads = jnp.concatenate([left[:, skel:], right[:, skel:]], axis=1)
            else:
                below = plan.upper_bases[level - 1]
                pair = jnp.concatenate([nodes[below + 2 * j], nodes[below + 2 * j + 1]], axis=1)
                coords, loads = pair[:dim], pair[depth:]
            matrix = jnp.concatenate(
                [gathered[j * group_size + k, offset : offset + rows] for k in range(group_size)], axis=0
            )
            place = pick(coords, all_ids[level][pl.ds(j, 1)])
            nodes[base + j, :dim] = place
            nodes[base + j, dim:depth] = norm_rows(place, 3)
            nodes[base + j, depth:] = nt(loads, matrix).astype(BF)
            return 0

        lax.fori_loop(0, n_nodes, one_node, 0, unroll=min(n_nodes, 8))
        offsets.append(offset)
        offset += rows

    for level in range(len(plan.upper_counts)):
        goals[level] = target_side(nodes[plan.upper_bases[level] + (position >> (level + 1)), :dim])
    acc[...] = jnp.zeros_like(acc)
    add_items(plan, table, 4, FAR_SIZES, goals, nodes, dim, scale, acc, plan.upper_row, lambda s: 0)

    total = None
    for level in range(len(plan.upper_counts) - 1, -1, -1):
        ancestor = position >> (level + 1)
        group_size = 2 << level
        rows = skel // group_size
        total = acc[level] if total is None else total + acc[level]
        branch = (position >> level) & 1
        cols = pl.ds(pl.multiple_of(branch * skel, skel), skel)
        matrix = jnp.concatenate(
            [
                gathered[ancestor * group_size + k, offsets[level] : offsets[level] + rows, cols]
                for k in range(group_size)
            ],
            axis=0,
        )
        total = through(total, matrix)

    firsts = []
    made = 0
    for degree in range(levels + 1):
        firsts.append(made)
        made += max(1, share >> degree)
    totals = [total + far[firsts[levels]]]
    for degree in range(levels, 0, -1):
        first_row = leaf_count - 2 * (leaf_count >> degree)
        start = (member * share) >> degree
        child_start = (member * share) >> (degree - 1)
        children = max(1, share >> (degree - 1))
        after = []
        if children == 1:
            branch = child_start & 1
            cols = pl.ds(pl.multiple_of(branch * skel, skel), skel)
            after.append(through(totals[0], inner_maps[first_row + start, :, cols]) + far[firsts[degree - 1]])
        else:
            for c in range(children // 2):
                both = through(totals[c], inner_maps[first_row + start + c])
                after.append(both[:, :skel] + far[firsts[degree - 1] + 2 * c])
                after.append(both[:, skel:] + far[firsts[degree - 1] + 2 * c + 1])
        totals = after
    for c in range(share):
        out[:, c * leaf_size : (c + 1) * leaf_size] = (
            through(totals[c], leaf_maps[member * share + c]) + near[c]
        )


def on_device(
    points,
    charges,
    leaf_ids,
    inner_ids,
    upper_ids_first,
    upper_ids_second,
    upper_ids_third,
    leaf_maps,
    inner_maps,
    upper_maps_first,
    upper_maps_second,
    upper_maps_third,
    near_lists,
    far_inner,
    far_upper_first,
    far_upper_second,
    far_upper_third,
):
    dim, local_points = points.shape
    rhs = charges.shape[0]
    leaf_count, skel, leaf_size = leaf_maps.shape
    levels = leaf_count.bit_length() - 1
    stacked = dim + rhs
    depth = dim + NORM_ROWS
    subtrees = lax.axis_size("leaf")
    list_size = lax.axis_size("list")
    share = leaf_count // list_size
    scale = -3.0 / dim * math.log2(math.e)
    rightward = [(i, i + 1) for i in range(subtrees - 1)]
    leftward = [(i + 1, i) for i in range(subtrees - 1)]

    spot = jnp.stack([lax.axis_index("leaf"), lax.axis_index("list")]).astype(jnp.int32)
    mine = jnp.concatenate(
        [near_lists, far_inner, far_upper_first, far_upper_second, far_upper_third], axis=0
    )
    chunks = [mine] + [
        lax.ppermute(mine, "list", [(i, (i + shift) % list_size) for i in range(list_size)])
        for shift in range(1, list_size)
    ]
    uppers = (far_upper_first, far_upper_second, far_upper_third)
    plan = Plan(leaf_count, share, levels, list_size * mine.shape[1], [a.shape[0] for a in uppers])

    vmem = pl.BlockSpec(memory_space=pltpu.VMEM)
    smem = pl.BlockSpec(memory_space=pltpu.SMEM)
    anywhere = pl.BlockSpec(memory_space=pl.ANY)
    params = pltpu.CompilerParams(vmem_limit_bytes=VMEM_BYTES)

    def shaped(shape, dtype=BF):
        return jax.ShapeDtypeStruct(shape, dtype)

    def cost(flops, transcendentals=0):
        return pl.CostEstimate(flops=flops, bytes_accessed=4 * 10**6, transcendentals=transcendentals)

    inputs = (points, charges, leaf_ids, inner_ids, leaf_maps, inner_maps, upper_maps_first, upper_maps_second, upper_maps_third)
    block_rows = dim + sum(a.shape[0] for a in inputs[6:])
    bundle, blocks = pl.pallas_call(
        functools.partial(up_body, levels),
        out_shape=(shaped((2 * leaf_count, stacked, leaf_size)), shaped((subtrees, block_rows, 2 * skel))),
        in_specs=[anywhere] * 9,
        out_specs=(vmem, vmem),
        scratch_shapes=[pltpu.VMEM(a.shape, a.dtype) for a in inputs] + [pltpu.SemaphoreType.DMA((9,))],
        compiler_params=pltpu.CompilerParams(vmem_limit_bytes=UP_VMEM_BYTES),
        name="upward",
        cost_estimate=cost(10**9),
    )(*inputs)

    left = lax.ppermute(bundle, "leaf", rightward)
    right = lax.ppermute(bundle, "leaf", leftward)
    gathered = lax.all_to_all(blocks, "leaf", split_axis=0, concat_axis=0, tiled=True)

    table = pl.pallas_call(
        functools.partial(table_body, plan, len(chunks)),
        out_shape=shaped((plan.out_rows, LANES), jnp.int32),
        in_specs=[smem] + [vmem] * len(chunks),
        out_specs=vmem,
        scratch_shapes=[pltpu.VMEM((LANES, LANES), jnp.int32)],
        compiler_params=params,
        name="table",
        cost_estimate=cost(10**9),
    )(spot, *chunks)

    acc_shapes = (shaped((share, rhs, leaf_size), F32), shaped((plan.targets, rhs, skel), F32))
    goal_shapes = (shaped((share, leaf_size, depth)), shaped((plan.targets, skel, depth)))

    def held(sides):
        return [
            pltpu.VMEM((sides * leaf_count, depth + rhs, leaf_size), BF),
            pltpu.VMEM((sides * plan.per_side, depth + rhs, skel), BF),
        ]

    near, far, near_goals, far_goals = pl.pallas_call(
        functools.partial(own_body, plan, dim, scale),
        out_shape=acc_shapes + goal_shapes,
        in_specs=[smem, smem, vmem],
        out_specs=(vmem,) * 4,
        scratch_shapes=held(1),
        compiler_params=params,
        name="own",
        cost_estimate=cost(10**10, 10**7),
    )(spot, table, bundle)

    near, far = pl.pallas_call(
        functools.partial(rim_body, plan, dim, scale),
        out_shape=acc_shapes,
        in_specs=[smem] + [vmem] * 6,
        out_specs=(vmem,) * 2,
        scratch_shapes=held(2),
        compiler_params=params,
        name="rim",
        cost_estimate=cost(2 * 10**10, 10**7),
    )(table, left, right, near, far, near_goals, far_goals)

    return pl.pallas_call(
        functools.partial(down_body, plan, dim, scale),
        out_shape=shaped((rhs, share * leaf_size), F32),
        in_specs=[smem, smem] + [vmem] * 8,
        out_specs=vmem,
        scratch_shapes=[
            pltpu.VMEM((sum(plan.upper_counts), depth + rhs, skel), BF),
            pltpu.VMEM((len(uppers), skel, depth), BF),
            pltpu.VMEM((len(uppers), rhs, skel), F32),
        ],
        compiler_params=params,
        name="down",
        cost_estimate=cost(10**9, 10**6),
    )(spot, table, gathered, upper_ids_first, upper_ids_second, upper_ids_third, far, near, inner_maps, leaf_maps)


def solution(mesh):
    placed = (
        P(None, "leaf"),
        P(None, "leaf"),
        P("leaf", None),
        P("leaf", None),
        P(),
        P(),
        P(),
        P("leaf", None, None),
        P("leaf", None, None),
        P("leaf", None),
        P("leaf", None),
        P("leaf", None),
        P("leaf", "list"),
        P("leaf", "list"),
        P(None, "list"),
        P(None, "list"),
        P(None, "list"),
    )
    return jax.shard_map(
        on_device, mesh=mesh, in_specs=placed, out_specs=P(None, ("leaf", "list")), check_vma=False
    )
```

profile of v0, /device:TPU:22, one launch (start us, length us, event | category | flops | bytes accessed | tf_op | source)
XLA Modules:
  0.0 65.2 jit_solution(10955493621344796978)
XLA Ops:
  0.0 0.0 copy-start.12
  0.0 0.0 copy-start.11
  0.0 4.1 %upward.1 = (bf16[32,64,256]{2,1,0:T(8,128)(2,1)}, bf16[16,144,256]{2,1,0:T(8,128)(2,1)}) custom-call(bf16[32,4096]{1,0:T(8,128)(2,1)} %refs_0_.1, bf16[32,4096]{1,0:T(8,128)(2,1)} %refs_1_.1, s32[16,128]{1,0:T(8,128)} %refs_2_.1, s32[15,128]{1,0:T(8,128)} %refs_3_.1, bf16[16,128,256]{2,1,0:T(8,128)(2,1)} %leaf_maps.1, bf16[15,128,256]{2,1,0:T(8,128)(2,1)} %inner_maps.1, ...), custom_call_target="tpu_custom_call" | custom-call | flops 1000000000 | bytes 4000000 | tf_op jit(solution)/shard_map/upward/pallas_call | solution.py:480
  4.2 1.9 %collective-permute-start.2 = (bf16[32,64,256]{2,1,0:T(8,128)(2,1)}, bf16[32,64,256]{2,1,0:T(8,128)(2,1)S(1)}, u32[]{:S(2)}, u32[]{:S(2)}) collective-permute-start(bf16[32,64,256]{2,1,0:T(8,128)(2,1)} %get-tuple-element.14.bundle), channel_id=1, source_target_pairs={{2,0},{4,2},{6,4},{8,6},{10,8},{12,10},{14,12},{16,14},{18,16},{20... | collective-permute-start | bytes 3145736 | tf_op jit(solution)/shard_map/ppermute | solution.py:492
  6.1 2.4 %collective-permute-start.1 = (bf16[32,64,256]{2,1,0:T(8,128)(2,1)}, bf16[32,64,256]{2,1,0:T(8,128)(2,1)}, u32[]{:S(2)}, u32[]{:S(2)}) collective-permute-start(bf16[32,64,256]{2,1,0:T(8,128)(2,1)} %get-tuple-element.14.bundle), channel_id=1, source_target_pairs={{0,2},{2,4},{4,6},{6,8},{8,10},{10,12},{12,14},{14,16},{16,18},{18... | collective-permute-start | bytes 3145736 | tf_op jit(solution)/shard_map/ppermute | solution.py:491
  8.5 0.0 copy-done.10
  8.5 0.1 copy.25
  8.6 0.0 copy-done.14
  8.6 0.0 copy-done.13
  8.6 0.0 copy-done.12
  8.6 0.0 copy-done.11
  8.6 0.2 concatenate.3.refs_0_
  8.8 0.6 collective-permute-start
  9.4 6.4 %all-to-all-start = ((bf16[16,144,256]{2,1,0:T(8,128)(2,1)}), bf16[16,144,256]{2,1,0:T(8,128)(2,1)S(1)}, u32[]{:S(2)}, u32[]{:S(2)}) async-start(bf16[16,144,256]{2,1,0:T(8,128)(2,1)} %get-tuple-element.13), calls=%async_computation | async-start | bytes 2359296 | tf_op jit(solution)/shard_map/all_to_all | solution.py:493
  15.8 0.1 pad_add_fusion.spot
  15.9 0.0 collective-permute-done.refs_1_
  15.9 1.9 %table.1 = s32[16,128]{1,0:T(8,128)S(1)} custom-call(s32[2]{0:T(128)S(1)} %pad_add_fusion.spot, s32[61,16]{1,0:T(8,128)S(1)} %concatenate.3.refs_0_, s32[61,16]{1,0:T(8,128)S(1)} %collective-permute-done.refs_1_), custom_call_target="tpu_custom_call" | custom-call | flops 1000000000 | bytes 4000000 | tf_op jit(solution)/shard_map/table/pallas_call | solution.py:495
  17.8 0.0 copy-done.9
  17.8 8.6 %own.1 = (f32[8,32,256]{2,1,0:T(8,128)S(1)}, f32[16,32,128]{2,1,0:T(8,128)S(1)}, bf16[8,256,48]{2,1,0:T(8,128)(2,1)S(1)}, bf16[16,128,48]{2,1,0:T(8,128)(2,1)S(1)}) custom-call(s32[2]{0:T(128)S(1)} %pad_add_fusion.spot, s32[16,128]{1,0:T(8,128)S(1)} %table.1, bf16[32,64,256]{2,1,0:T(8,128)(2,1)S(1)} %copy-done.9), custom_call_target="tpu_custom_call" | custom-call | flops 10000000000 | bytes 4000000 | tf_op jit(solution)/shard_map/own/pallas_call | solution.py:515
  26.4 11.5 %collective-permute-done.2.right = bf16[32,64,256]{2,1,0:T(8,128)(2,1)S(1)} collective-permute-done((bf16[32,64,256]{2,1,0:T(8,128)(2,1)}, bf16[32,64,256]{2,1,0:T(8,128)(2,1)S(1)}, u32[]{:S(2)}, u32[]{:S(2)}) %collective-permute-start.2) | collective-permute-done | bytes 1048608 | tf_op jit(solution)/shard_map/ppermute | solution.py:492
  37.9 1.0 %copy-done.7 = bf16[32,64,256]{2,1,0:T(8,128)(2,1)} copy-done((bf16[32,64,256]{2,1,0:T(8,128)(2,1)}, bf16[32,64,256]{2,1,0:T(8,128)(2,1)S(1)}, u32[]{:S(2)}) %copy-start.7) | copy-done | bytes 1048600
  38.8 5.0 %collective-permute-done.1.left = bf16[32,64,256]{2,1,0:T(8,128)(2,1)} collective-permute-done((bf16[32,64,256]{2,1,0:T(8,128)(2,1)}, bf16[32,64,256]{2,1,0:T(8,128)(2,1)}, u32[]{:S(2)}, u32[]{:S(2)}) %collective-permute-start.1) | collective-permute-done | bytes 1048608 | tf_op jit(solution)/shard_map/ppermute | solution.py:491
  43.8 1.2 %copy-done.8 = bf16[32,64,256]{2,1,0:T(8,128)(2,1)S(1)} copy-done((bf16[32,64,256]{2,1,0:T(8,128)(2,1)S(1)}, bf16[32,64,256]{2,1,0:T(8,128)(2,1)}, u32[]{:S(2)}) %copy-start.8) | copy-done | bytes 1048600
  45.0 0.0 copy-start.6
  45.0 14.3 %rim.1 = (f32[8,32,256]{2,1,0:T(8,128)S(1)}, f32[16,32,128]{2,1,0:T(8,128)S(1)}) custom-call(s32[16,128]{1,0:T(8,128)S(1)} %table.1, bf16[32,64,256]{2,1,0:T(8,128)(2,1)} %collective-permute-done.1.left, bf16[32,64,256]{2,1,0:T(8,128)(2,1)S(1)} %copy-done.8, f32[8,32,256]{2,1,0:T(8,128)S(1)} %get-tuple-element.15.near_in, ...), custom_call_target="tpu_custom_call" | custom-call | flops 20000000000 | bytes 4000000 | tf_op jit(solution)/shard_map/rim/pallas_call | solution.py:526
  59.3 0.7 %copy-done.2 = f32[16,32,128]{2,1,0:T(8,128)} copy-done((f32[16,32,128]{2,1,0:T(8,128)}, f32[16,32,128]{2,1,0:T(8,128)S(1)}, u32[]{:S(2)}) %copy-start.2) | copy-done | bytes 262168
  60.1 0.0 all-to-all-done.gathered
  60.1 0.0 copy-done
  60.1 0.0 copy-done.1
  60.1 0.0 copy-done.4
  60.1 0.9 %copy-done.3 = f32[16,32,128]{2,1,0:T(8,128)S(1)} copy-done((f32[16,32,128]{2,1,0:T(8,128)S(1)}, f32[16,32,128]{2,1,0:T(8,128)}, u32[]{:S(2)}) %copy-start.3) | copy-done | bytes 262168
  61.0 4.1 %down.1 = f32[32,2048]{1,0:T(8,128)} custom-call(s32[2]{0:T(128)S(1)} %pad_add_fusion.spot, s32[16,128]{1,0:T(8,128)S(1)} %table.1, bf16[16,144,256]{2,1,0:T(8,128)(2,1)S(1)} %all-to-all-done.gathered, s32[8,128]{1,0:T(8,128)S(1)} %copy-done.4, s32[4,128]{1,0:T(4,128)S(1)} %copy-done.5, s32[2,128]{1,0:T(2,128)S(1)} %copy-done.6, ...), custom_call_target="tpu_custom_call" | custom-call | flops 1000000000 | bytes 4000000 | tf_op jit(solution)/shard_map/down/pallas_call | solution.py:537
  (14 shorter events, 0.0 us)
Async XLA Ops:
  0.0 8.5 %copy-start.10 = (s32[31,16]{0,1:T(8,128)S(1)}, s32[31,16]{0,1:T(8,128)}, u32[]{:S(2)}) copy-start(s32[31,16]{0,1:T(8,128)} %param.30) | copy-start | bytes 5956
  0.0 8.6 %copy-start.14 = (s32[2,16]{1,0:T(2,128)S(1)}, s32[2,16]{1,0:T(2,128)}, u32[]{:S(2)}) copy-start(s32[2,16]{1,0:T(2,128)} %param.33) | copy-start | bytes 388
  0.0 8.6 %copy-start.13 = (s32[4,16]{1,0:T(4,128)S(1)}, s32[4,16]{1,0:T(4,128)}, u32[]{:S(2)}) copy-start(s32[4,16]{1,0:T(4,128)} %param.32) | copy-start | bytes 772
  0.0 8.6 %copy-start.12 = (s32[8,16]{1,0:T(8,128)S(1)}, s32[8,16]{1,0:T(8,128)}, u32[]{:S(2)}) copy-start(s32[8,16]{1,0:T(8,128)} %param.31) | copy-start | bytes 1540
  0.0 8.6 %copy-start.11 = (s32[16,16]{1,0:T(8,128)S(1)}, s32[16,16]{1,0:T(8,128)}, u32[]{:S(2)}) copy-start(s32[16,16]{1,0:T(8,128)} %param.29) | copy-start | bytes 3076
  4.2 33.7 %collective-permute-start.2 = (bf16[32,64,256]{2,1,0:T(8,128)(2,1)}, bf16[32,64,256]{2,1,0:T(8,128)(2,1)S(1)}, u32[]{:S(2)}, u32[]{:S(2)}) collective-permute-start(bf16[32,64,256]{2,1,0:T(8,128)(2,1)} %get-tuple-element.14.bundle), channel_id=1, source_target_pairs={{2,0},{4,2},{6,4},{8,6},{10,8},{12,10},{14,12},{16,14},{18,16},{20... | collective-permute-start | bytes 3145736 | tf_op jit(solution)/shard_map/ppermute | solution.py:492
  6.1 37.7 %collective-permute-start.1 = (bf16[32,64,256]{2,1,0:T(8,128)(2,1)}, bf16[32,64,256]{2,1,0:T(8,128)(2,1)}, u32[]{:S(2)}, u32[]{:S(2)}) collective-permute-start(bf16[32,64,256]{2,1,0:T(8,128)(2,1)} %get-tuple-element.14.bundle), channel_id=1, source_target_pairs={{0,2},{2,4},{4,6},{6,8},{8,10},{10,12},{12,14},{14,16},{16,18},{18... | collective-permute-start | bytes 3145736 | tf_op jit(solution)/shard_map/ppermute | solution.py:491
  8.8 7.1 %collective-permute-start = (s32[61,16]{1,0:T(8,128)S(1)}, s32[61,16]{1,0:T(8,128)S(1)}, u32[]{:S(2)}, u32[]{:S(2)}) collective-permute-start(s32[61,16]{1,0:T(8,128)S(1)} %concatenate.3.refs_0_), channel_id=1, source_target_pairs={{0,1},{1,0},{2,3},{3,2},{4,5},{5,4},{6,7},{7,6},{8,9},{9,8},{10,11... | collective-permute-start | bytes 11720 | tf_op jit(solution)/shard_map/ppermute | solution.py:461
  9.4 50.6 %all-to-all-start = ((bf16[16,144,256]{2,1,0:T(8,128)(2,1)}), bf16[16,144,256]{2,1,0:T(8,128)(2,1)S(1)}, u32[]{:S(2)}, u32[]{:S(2)}) async-start(bf16[16,144,256]{2,1,0:T(8,128)(2,1)} %get-tuple-element.13), calls=%async_computation | async-start | bytes 2359296 | tf_op jit(solution)/shard_map/all_to_all | solution.py:493
  15.9 1.9 %copy-start.9 = (bf16[32,64,256]{2,1,0:T(8,128)(2,1)S(1)}, bf16[32,64,256]{2,1,0:T(8,128)(2,1)}, u32[]{:S(2)}) copy-start(bf16[32,64,256]{2,1,0:T(8,128)(2,1)} %get-tuple-element.14.bundle) | copy-start | bytes 3145732
  37.9 1.0 %copy-start.7 = (bf16[32,64,256]{2,1,0:T(8,128)(2,1)}, bf16[32,64,256]{2,1,0:T(8,128)(2,1)S(1)}, u32[]{:S(2)}) copy-start(bf16[32,64,256]{2,1,0:T(8,128)(2,1)S(1)} %collective-permute-done.2.right) | copy-start | bytes 3145732
  43.8 1.2 %copy-start.8 = (bf16[32,64,256]{2,1,0:T(8,128)(2,1)S(1)}, bf16[32,64,256]{2,1,0:T(8,128)(2,1)}, u32[]{:S(2)}) copy-start(bf16[32,64,256]{2,1,0:T(8,128)(2,1)} %copy-done.7) | copy-start | bytes 3145732
  45.0 15.0 %copy-start = (bf16[16,128,256]{2,1,0:T(8,128)(2,1)S(1)}, bf16[16,128,256]{2,1,0:T(8,128)(2,1)}, u32[]{:S(2)}) copy-start(bf16[16,128,256]{2,1,0:T(8,128)(2,1)} %leaf_maps.1) | copy-start | bytes 3145732
  45.0 15.0 %copy-start.1 = (bf16[15,128,256]{2,1,0:T(8,128)(2,1)S(1)}, bf16[15,128,256]{2,1,0:T(8,128)(2,1)}, u32[]{:S(2)}) copy-start(bf16[15,128,256]{2,1,0:T(8,128)(2,1)} %inner_maps.1) | copy-start | bytes 2949124
  45.0 15.0 %copy-start.4 = (s32[8,128]{1,0:T(8,128)S(1)}, s32[8,128]{1,0:T(8,128)}, u32[]{:S(2)}) copy-start(s32[8,128]{1,0:T(8,128)} %ids1.1) | copy-start | bytes 12292
  45.0 15.0 %copy-start.5 = (s32[4,128]{1,0:T(4,128)S(1)}, s32[4,128]{1,0:T(4,128)}, u32[]{:S(2)}) copy-start(s32[4,128]{1,0:T(4,128)} %ids2.1) | copy-start | bytes 6148
  45.0 15.1 %copy-start.6 = (s32[2,128]{1,0:T(2,128)S(1)}, s32[2,128]{1,0:T(2,128)}, u32[]{:S(2)}) copy-start(s32[2,128]{1,0:T(2,128)} %ids3.1) | copy-start | bytes 3076
  59.3 0.7 %copy-start.2 = (f32[16,32,128]{2,1,0:T(8,128)}, f32[16,32,128]{2,1,0:T(8,128)S(1)}, u32[]{:S(2)}) copy-start(f32[16,32,128]{2,1,0:T(8,128)S(1)} %get-tuple-element.19.far) | copy-start | bytes 786436
  60.1 1.0 %copy-start.3 = (f32[16,32,128]{2,1,0:T(8,128)S(1)}, f32[16,32,128]{2,1,0:T(8,128)}, u32[]{:S(2)}) copy-start(f32[16,32,128]{2,1,0:T(8,128)} %copy-done.2) | copy-start | bytes 786436
where the time goes:
time: 65.9 us; the launch traced here: 65.2 us
  Pallas kernels  33 us (50%)
  waiting for transfers between devices  16.5 us (25%)
  starting transfers between devices  11.3 us (17%)
  local copies, waits for them, and re-layouts  4.19 us (6%)
    pallas_call x1, Pallas kernels, on_device(): pl.pallas_call(functools.partial(rim_body, plan, dim, scale), out_shape=a...  14.3 us
    ppermute x1, waiting for transfers between devices, on_device(): right = lax.ppermute(bundle, 'leaf', leftward)  11.5 us
    pallas_call x1, Pallas kernels, on_device(): pl.pallas_call(functools.partial(own_body, plan, dim, scale), out_shape=a...  8.57 us
    all_to_all x1, starting transfers between devices, on_device(): lax.all_to_all(blocks, 'leaf', split_axis=0, concat_axis=0, tiled=True)  6.41 us
    ppermute x1, waiting for transfers between devices, on_device(): left = lax.ppermute(bundle, 'leaf', rightward)  4.95 us
    pallas_call x1, Pallas kernels, on_device(): pl.pallas_call(functools.partial(down_body, plan, dim, scale), out_shape=...  4.13 us
    pallas_call x1, Pallas kernels, on_device(): pl.pallas_call(functools.partial(up_body, levels), out_shape=(shaped((2 *...  4.12 us
    unnamed x31, local copies, waits for them, and re-layouts  3.98 us
  transfers between devices with their start and end apart: 4, of which 2 were waited for; matrix products, arithmetic and copies ran while one was open for 1% of the time, Pallas kernels for 38%

commit v1 on v0

--- a/solution.py
+++ b/solution.py
@@ -120,8 +120,8 @@
         copies[i].wait()
         parts.append(held[i][...])
     whole = jnp.concatenate(parts, axis=0)
-    for device in range(blocks.shape[0]):
-        blocks[device] = whole
+    for i in range(blocks.shape[0]):
+        blocks[i] = whole
 
 
 def ceil_to(value, unit):
@@ -131,7 +131,7 @@
 class Plan:
     def __init__(self, leaf_count, share, levels, slots, upper_counts):
         self.leaf_count, self.share, self.levels, self.slots = leaf_count, share, levels, slots
-        self.per_side = 2 * leaf_count - 1
+        self.per_side = 2 * leaf_count
         self.counts = [max(1, share >> degree) for degree in range(levels + 1)]
         self.first_rows = [2 * leaf_count - 2 * (leaf_count >> degree) for degree in range(levels + 1)]
         self.targets = sum(self.counts)
@@ -145,10 +145,10 @@
             return ceil_to(min(slots, count), unit)
 
         most = [
+            share * room(2 * leaf_count, NEAR_UNIT),
             share * room(leaf_count, NEAR_UNIT),
-            share * room(2 * leaf_count, NEAR_UNIT),
+            sum(c * room(2 * t, FAR_UNIT) for c, t in zip(self.counts, trees)),
             sum(c * room(t, FAR_UNIT) for c, t in zip(self.counts, trees)),
-            sum(c * room(2 * t, FAR_UNIT) for c, t in zip(self.counts, trees)),
             sum(room(c, FAR_UNIT) for c in upper_counts),
         ]
         self.starts, at = [], 0
@@ -160,6 +160,9 @@
         width = max(3 * leaf_count, 3 * self.per_side, sum(upper_counts))
         assert width <= LANES and self.rows <= LANES and slots <= LANES
 
+    def node_at(self, node):
+        return (node & 1) * self.leaf_count + (node >> 1)
+
 
 def table_body(plan, n_chunks, spot, *refs):
     chunks, (out, held) = refs[:n_chunks], refs[n_chunks:]
@@ -170,19 +173,23 @@
     def rows_of(start, count):
         return jnp.concatenate([chunk[pl.ds(start, count)] for chunk in chunks], axis=1)
 
+    def split(entries, shift):
+        tree = entries >> shift
+        side = jnp.where(tree == position, 0, jnp.where(tree == (position ^ 1), 1, 2))
+        return side, entries & ((1 << shift) - 1)
+
     slots = plan.slots
     entries = rows_of(member * share, share)
-    held[:share, :slots] = jnp.where(entries >= 0, entries - (position - 1) * leaf_count, -1)
+    side, within = split(entries, plan.levels)
+    held[:share, :slots] = jnp.where(entries >= 0, side * leaf_count + within, -1)
     row = plan.far_row
     for degree in range(plan.levels + 1):
         count = plan.counts[degree]
-        shift = plan.levels - degree
         entries = rows_of(leaf_count + plan.first_rows[degree] + ((member * share) >> degree), count)
-        side = (entries >> shift) - position + 1
-        within = entries & ((1 << shift) - 1)
-        held[row : row + count, :slots] = side * plan.per_side + plan.first_rows[degree] + within
+        side, within = split(entries, plan.levels - degree)
+        held[row : row + count, :slots] = side * plan.per_side + plan.node_at(plan.first_rows[degree] + within)
         row += count
-    at = leaf_count + plan.per_side
+    at = leaf_count + plan.per_side - 1
     for level, count in enumerate(plan.upper_counts):
         entries = rows_of(at + (position >> (level + 1)), 1)
         held[row : row + 1, :slots] = entries + plan.upper_bases[level]
@@ -199,7 +206,7 @@
         often += jnp.where(across[k : k + 1] == source, 1.0, 0.0)
     near_r, far_r = plan.far_row, plan.upper_row
     half = jnp.where(across_i < near_r, leaf_count, plan.per_side)
-    inside = (down_i >= half) & (down_i < 2 * half)
+    inside = down_i < 2 * half
     own = (inside & (across_i < far_r)) | ((across_i >= far_r) & (across_i < plan.rows))
     present = often > 0.0
     is_own = jnp.where(present & own, 1.0, 0.0)
@@ -258,7 +265,7 @@
     return code & (LANES - 1), ((code >> 7) & 63).astype(F32), code >> 13
 
 
-def add_items(plan, table, kind, sizes, goals, nodes, dim, scale, acc, first_row, source_base):
+def add_items(plan, table, kind, sizes, goals, nodes, dim, scale, acc, first_row, first_source):
     unit, unroll = sizes
     depth = dim + NORM_ROWS
     start = plan.starts[kind]
@@ -269,7 +276,7 @@
         terms = []
         for k in range(unroll):
             items = [decode(table, start + step * group + k * unit + u) for u in range(unit)]
-            sources = [jnp.maximum(item[0] - source_base(item[0]), 0) for item in items]
+            sources = [jnp.maximum(item[0] - first_source, 0) for item in items]
             row = jnp.maximum(items[0][2] - first_row, 0)
             places = jnp.concatenate([nodes[source, :depth] for source in sources], axis=1)
             block = jnp.exp2(nn(goals[row], places) * scale)
@@ -288,59 +295,117 @@
     lax.fori_loop(0, (total + group - 1) // group, some, 0)
 
 
-def load_leaf(nodes, at, both, dim):
-    nodes[at, :dim] = both[:dim]
-    nodes[at, dim : dim + NORM_ROWS] = norm_rows(both[:dim], 3)
-    nodes[at, dim + NORM_ROWS :] = both[dim:]
-
-
-def load_side(plan, bundle, leaves, nodes, leaf_at, node_at, dim):
+def leaf_copies(plan, bundle, leaves, at, dim, sems):
+    some = slice(0, plan.leaf_count)
+    there = pl.ds(at, plan.leaf_count)
+    return [
+        pltpu.make_async_copy(bundle.at[some, 0:dim], leaves.at[there, 0:dim], sems.at[0]),
+        pltpu.make_async_copy(bundle.at[some, dim:], leaves.at[there, dim + NORM_ROWS :], sems.at[1]),
+    ]
+
+
+def node_copies(plan, bundle, nodes, at, dim, sems):
+    count = plan.leaf_count
     skel = nodes.shape[2]
-    for i in range(plan.leaf_count):
-        load_leaf(leaves, leaf_at + i, bundle[i], dim)
-    for i in range(plan.per_side):
-        cols = slice((i % 2) * skel, (i % 2 + 1) * skel)
-        load_leaf(nodes, node_at + i, bundle[plan.leaf_count + i // 2, :, cols], dim)
-
-
-def own_body(plan, dim, scale, spot, table, bundle, near, far, near_goals, far_goals, leaves, nodes):
+    copies = []
+    for odd in range(2):
+        there = pl.ds(at + odd * count, count)
+        cols = slice(odd * skel, (odd + 1) * skel)
+        copies += [
+            pltpu.make_async_copy(bundle.at[count : 2 * count, 0:dim, cols], nodes.at[there, 0:dim], sems.at[2 * odd]),
+            pltpu.make_async_copy(
+                bundle.at[count : 2 * count, dim:, cols], nodes.at[there, dim + NORM_ROWS :], sems.at[2 * odd + 1]
+            ),
+        ]
+    return copies
+
+
+def run_copies(copies):
+    for copy in copies:
+        copy.start()
+    for copy in copies:
+        copy.wait()
+
+
+def fill_norms(nodes, dim):
+    for i in range(nodes.shape[0]):
+        nodes[i, dim : dim + NORM_ROWS] = norm_rows(nodes[i, :dim], 3)
+
+
+def near_body(plan, dim, scale, spot, table, bundle, pair, column, near, goals, joined, leaves, sems, column_sem):
+    move = pltpu.make_async_copy(column, joined, column_sem)
+    move.start()
     member = spot[1]
-    leaf_count, share = plan.leaf_count, plan.share
-    load_side(plan, bundle, leaves, nodes, 0, 0, dim)
+    count, share = plan.leaf_count, plan.share
+    run_copies(
+        leaf_copies(plan, bundle, leaves, 0, dim, sems.at[0]) + leaf_copies(plan, pair, leaves, count, dim, sems.at[1])
+    )
+    fill_norms(leaves, dim)
     for t in range(share):
-        near_goals[t] = target_side(leaves[member * share + t, :dim])
+        goals[t] = target_side(leaves[member * share + t, :dim])
+    near[...] = jnp.zeros_like(near)
+    add_items(plan, table, 0, NEAR_SIZES, goals, leaves, dim, scale, near, 0, 0)
+    move.wait()
+
+
+def far_body(plan, dim, scale, spot, table, bundle, pair, far, goals, nodes, sems):
+    member = spot[1]
+    run_copies(
+        node_copies(plan, bundle, nodes, 0, dim, sems.at[0])
+        + node_copies(plan, pair, nodes, plan.per_side, dim, sems.at[1])
+    )
+    fill_norms(nodes, dim)
     made = 0
     for degree in range(plan.levels + 1):
-        start = plan.first_rows[degree] + ((member * share) >> degree)
+        start = plan.first_rows[degree] + ((member * plan.share) >> degree)
         for t in range(plan.counts[degree]):
-            far_goals[made + t] = target_side(nodes[start + t, :dim])
+            goals[made + t] = target_side(nodes[plan.node_at(start + t), :dim])
         made += plan.counts[degree]
-    near[...] = jnp.zeros_like(near)
     far[...] = jnp.zeros_like(far)
-    add_items(plan, table, 0, NEAR_SIZES, near_goals, leaves, dim, scale, near, 0, lambda s: leaf_count)
-    add_items(plan, table, 2, FAR_SIZES, far_goals, nodes, dim, scale, far, plan.far_row, lambda s: plan.per_side)
-
-
-def rim_body(plan, dim, scale, table, left, right, near_in, far_in, near_goals, far_goals, near, far, leaves, nodes):
-    leaf_count, per_side = plan.leaf_count, plan.per_side
-    load_side(plan, left, leaves, nodes, 0, 0, dim)
-    load_side(plan, right, leaves, nodes, leaf_count, per_side, dim)
+    add_items(plan, table, 2, FAR_SIZES, goals, nodes, dim, scale, far, plan.far_row, 0)
+
+
+def cross_far_body(plan, dim, scale, table, cross, far_in, goals, part, far, passed, nodes, sems, part_sem):
+    move = pltpu.make_async_copy(part, passed, part_sem)
+    move.start()
+    run_copies(node_copies(plan, cross, nodes, 0, dim, sems))
+    fill_norms(nodes, dim)
+    far[...] = far_in[...]
+    add_items(plan, table, 3, FAR_SIZES, goals, nodes, dim, scale, far, plan.far_row, 2 * plan.per_side)
+    move.wait()
+
+
+def cross_near_body(plan, dim, scale, table, cross, near_in, goals, part, near, leaves, sems):
+    run_copies(leaf_copies(plan, cross, leaves, 0, dim, sems))
+    fill_norms(leaves, dim)
     near[...] = near_in[...]
-    far[...] = far_in[...]
-
-    def rim(count):
-        return lambda s: jnp.where(s >= 2 * count, count, 0)
-
-    add_items(plan, table, 1, NEAR_SIZES, near_goals, leaves, dim, scale, near, 0, rim(leaf_count))
-    add_items(plan, table, 3, FAR_SIZES, far_goals, nodes, dim, scale, far, plan.far_row, rim(per_side))
-
-
-def down_body(plan, dim, scale, spot, table, gathered, ids1, ids2, ids3, far, near, inner_maps, leaf_maps, out, nodes, goals, acc):
+    add_items(plan, table, 1, NEAR_SIZES, goals, leaves, dim, scale, near, 0, 2 * plan.leaf_count)
+
+
+def down_body(plan, dim, scale, spot, table, *refs):
+    quarters, refs = refs[:4], refs[4:]
+    ids1, ids2, ids3, far, near, inner_maps, leaf_maps, out, nodes, goals, acc, gathered, where_is, sems = refs
+    quarter = quarters[0].shape[0]
+    copies = [
+        pltpu.make_async_copy(part, gathered.at[i * quarter : (i + 1) * quarter], sems.at[i])
+        for i, part in enumerate(quarters)
+    ]
+    for copy in copies:
+        copy.start()
     leaf_count, skel, leaf_size = leaf_maps.shape
     share, levels = plan.share, plan.levels
     depth = dim + NORM_ROWS
     position, member = spot[0], spot[1]
     all_ids = (ids1, ids2, ids3)
+
+    def find(d, _):
+        other = d ^ position
+        where_is[d] = (other & 3) * quarter + (d >> 2)
+        return 0
+
+    lax.fori_loop(0, gathered.shape[0], find, 0, unroll=16)
+    for copy in copies:
+        copy.wait()
 
     offsets = []
     offset = dim
@@ -351,7 +416,7 @@
 
         def one_node(j, _, level=level, base=base, offset=offset, group_size=group_size, rows=rows):
             if level == 0:
-                left, right = gathered[2 * j, :dim], gathered[2 * j + 1, :dim]
+                left, right = gathered[where_is[2 * j], :dim], gathered[where_is[2 * j + 1], :dim]
                 coords = jnp.concatenate([left[:, :skel], right[:, :skel]], axis=1)
                 loads = jnp.concatenate([left[:, skel:], right[:, skel:]], axis=1)
             else:
@@ -359,7 +424,7 @@
                 pair = jnp.concatenate([nodes[below + 2 * j], nodes[below + 2 * j + 1]], axis=1)
                 coords, loads = pair[:dim], pair[depth:]
             matrix = jnp.concatenate(
-                [gathered[j * group_size + k, offset : offset + rows] for k in range(group_size)], axis=0
+                [gathered[where_is[j * group_size + k], offset : offset + rows] for k in range(group_size)], axis=0
             )
             place = pick(coords, all_ids[level][pl.ds(j, 1)])
             nodes[base + j, :dim] = place
@@ -374,7 +439,7 @@
     for level in range(len(plan.upper_counts)):
         goals[level] = target_side(nodes[plan.upper_bases[level] + (position >> (level + 1)), :dim])
     acc[...] = jnp.zeros_like(acc)
-    add_items(plan, table, 4, FAR_SIZES, goals, nodes, dim, scale, acc, plan.upper_row, lambda s: 0)
+    add_items(plan, table, 4, FAR_SIZES, goals, nodes, dim, scale, acc, plan.upper_row, 0)
 
     total = None
     for level in range(len(plan.upper_counts) - 1, -1, -1):
@@ -386,7 +451,7 @@
         cols = pl.ds(pl.multiple_of(branch * skel, skel), skel)
         matrix = jnp.concatenate(
             [
-                gathered[ancestor * group_size + k, offsets[level] : offsets[level] + rows, cols]
+                gathered[where_is[ancestor * group_size + k], offsets[level] : offsets[level] + rows, cols]
                 for k in range(group_size)
             ],
             axis=0,
@@ -450,8 +515,8 @@
     list_size = lax.axis_size("list")
     share = leaf_count // list_size
     scale = -3.0 / dim * math.log2(math.e)
-    rightward = [(i, i + 1) for i in range(subtrees - 1)]
-    leftward = [(i + 1, i) for i in range(subtrees - 1)]
+    on_chip = [(i, i ^ 1) for i in range(subtrees)]
+    across = [pair for i in range(1, subtrees - 1, 2) for pair in ((i, i + 1), (i + 1, i))]
 
     spot = jnp.stack([lax.axis_index("leaf"), lax.axis_index("list")]).astype(jnp.int32)
     mine = jnp.concatenate(
@@ -479,7 +544,7 @@
     block_rows = dim + sum(a.shape[0] for a in inputs[6:])
     bundle, blocks = pl.pallas_call(
         functools.partial(up_body, levels),
-        out_shape=(shaped((2 * leaf_count, stacked, leaf_size)), shaped((subtrees, block_rows, 2 * skel))),
+        out_shape=(shaped((2 * leaf_count, stacked, leaf_size)), shaped((subtrees // 4, block_rows, 2 * skel))),
         in_specs=[anywhere] * 9,
         out_specs=(vmem, vmem),
         scratch_shapes=[pltpu.VMEM(a.shape, a.dtype) for a in inputs] + [pltpu.SemaphoreType.DMA((9,))],
@@ -488,9 +553,10 @@
         cost_estimate=cost(10**9),
     )(*inputs)
 
-    left = lax.ppermute(bundle, "leaf", rightward)
-    right = lax.ppermute(bundle, "leaf", leftward)
-    gathered = lax.all_to_all(blocks, "leaf", split_axis=0, concat_axis=0, tiled=True)
+    cross = lax.ppermute(bundle, "leaf", across)
+    pair = lax.ppermute(bundle, "leaf", on_chip)
+    columns = [list(range(i, subtrees, 4)) for i in range(4)]
+    column = lax.all_to_all(blocks, "leaf", split_axis=0, concat_axis=0, tiled=True, axis_index_groups=columns)
 
     table = pl.pallas_call(
         functools.partial(table_body, plan, len(chunks)),
@@ -506,48 +572,80 @@
     acc_shapes = (shaped((share, rhs, leaf_size), F32), shaped((plan.targets, rhs, skel), F32))
     goal_shapes = (shaped((share, leaf_size, depth)), shaped((plan.targets, skel, depth)))
 
-    def held(sides):
-        return [
-            pltpu.VMEM((sides * leaf_count, depth + rhs, leaf_size), BF),
-            pltpu.VMEM((sides * plan.per_side, depth + rhs, skel), BF),
-        ]
-
-    near, far, near_goals, far_goals = pl.pallas_call(
-        functools.partial(own_body, plan, dim, scale),
-        out_shape=acc_shapes + goal_shapes,
-        in_specs=[smem, smem, vmem],
-        out_specs=(vmem,) * 4,
-        scratch_shapes=held(1),
+    def leaves_of(sides):
+        return pltpu.VMEM((sides * leaf_count, depth + rhs, leaf_size), BF)
+
+    def nodes_of(sides):
+        return pltpu.VMEM((sides * plan.per_side, depth + rhs, skel), BF)
+
+    near, near_goals, joined = pl.pallas_call(
+        functools.partial(near_body, plan, dim, scale),
+        out_shape=(acc_shapes[0], goal_shapes[0], shaped(column.shape)),
+        in_specs=[smem, smem] + [anywhere] * 3,
+        out_specs=(vmem, vmem, anywhere),
+        scratch_shapes=[leaves_of(2), pltpu.SemaphoreType.DMA((2, 2)), pltpu.SemaphoreType.DMA],
         compiler_params=params,
-        name="own",
+        name="near",
         cost_estimate=cost(10**10, 10**7),
-    )(spot, table, bundle)
-
-    near, far = pl.pallas_call(
-        functools.partial(rim_body, plan, dim, scale),
-        out_shape=acc_shapes,
-        in_specs=[smem] + [vmem] * 6,
+    )(spot, table, bundle, pair, column)
+
+    def swapped(value, mask):
+        return lax.ppermute(value, "leaf", [(i, i ^ mask) for i in range(subtrees)])
+
+    second, third = swapped(joined, 1), swapped(joined, 2)
+
+    far, far_goals = pl.pallas_call(
+        functools.partial(far_body, plan, dim, scale),
+        out_shape=(acc_shapes[1], goal_shapes[1]),
+        in_specs=[smem, smem, anywhere, anywhere],
         out_specs=(vmem,) * 2,
-        scratch_shapes=held(2),
+        scratch_shapes=[nodes_of(2), pltpu.SemaphoreType.DMA((2, 4))],
         compiler_params=params,
-        name="rim",
-        cost_estimate=cost(2 * 10**10, 10**7),
-    )(table, left, right, near, far, near_goals, far_goals)
+        name="far",
+        cost_estimate=cost(10**10, 10**7),
+    )(spot, table, bundle, pair)
+
+    far, passed = pl.pallas_call(
+        functools.partial(cross_far_body, plan, dim, scale),
+        out_shape=(acc_shapes[1], shaped(third.shape)),
+        in_specs=[smem, anywhere, vmem, vmem, anywhere],
+        out_specs=(vmem, anywhere),
+        scratch_shapes=[nodes_of(1), pltpu.SemaphoreType.DMA((4,)), pltpu.SemaphoreType.DMA],
+        compiler_params=params,
+        name="crossfar",
+        cost_estimate=cost(10**10, 10**7),
+    )(table, cross, far, far_goals, third)
+
+    quarters = [joined, second, third, swapped(passed, 1)]
+
+    near = pl.pallas_call(
+        functools.partial(cross_near_body, plan, dim, scale),
+        out_shape=acc_shapes[0],
+        in_specs=[smem, anywhere, vmem, vmem, anywhere],
+        out_specs=vmem,
+        scratch_shapes=[leaves_of(1), pltpu.SemaphoreType.DMA((2,))],
+        compiler_params=params,
+        name="crossnear",
+        cost_estimate=cost(10**10, 10**7),
+    )(table, cross, near, near_goals, passed)
 
     return pl.pallas_call(
         functools.partial(down_body, plan, dim, scale),
         out_shape=shaped((rhs, share * leaf_size), F32),
-        in_specs=[smem, smem] + [vmem] * 8,
+        in_specs=[smem, smem] + [anywhere] * 4 + [vmem] * 7,
         out_specs=vmem,
         scratch_shapes=[
             pltpu.VMEM((sum(plan.upper_counts), depth + rhs, skel), BF),
             pltpu.VMEM((len(uppers), skel, depth), BF),
             pltpu.VMEM((len(uppers), rhs, skel), F32),
+            pltpu.VMEM((subtrees, block_rows, 2 * skel), BF),
+            pltpu.SMEM((subtrees,), jnp.int32),
+            pltpu.SemaphoreType.DMA((4,)),
         ],
         compiler_params=params,
         name="down",
         cost_estimate=cost(10**9, 10**6),
-    )(spot, table, gathered, upper_ids_first, upper_ids_second, upper_ids_third, far, near, inner_maps, leaf_maps)
+    )(spot, table, *quarters, upper_ids_first, upper_ids_second, upper_ids_third, far, near, inner_maps, leaf_maps)
 
 
 def solution(mesh):

time: 65.9 us -> 58.9 us (0.89)
  the two profiles are of different devices: /device:TPU:22 before, /device:TPU:11 now
where the time goes in v1:
time: 58.9 us; the launch traced here: 58.5 us
  Pallas kernels  33 us (56%)
  starting transfers between devices  13.9 us (24%)
  waiting for transfers between devices  10.4 us (18%)
  local copies, waits for them, and re-layouts  0.94 us (2%)
    pallas_call x1, Pallas kernels, on_device(): pl.pallas_call(functools.partial(far_body, plan, dim, scale), out_shape=(...  7.05 us
    pallas_call x1, Pallas kernels, on_device(): pl.pallas_call(functools.partial(near_body, plan, dim, scale), out_shape=...  6.67 us
    ppermute x1, waiting for transfers between devices, on_device(): cross = lax.ppermute(bundle, 'leaf', across)  5.31 us
    pallas_call x1, Pallas kernels, on_device(): pl.pallas_call(functools.partial(cross_near_body, plan, dim, scale), out_...  4.91 us
    all_to_all x1, starting transfers between devices, on_device(): lax.all_to_all(blocks, 'leaf', split_axis=0, concat_axis=0, tiled=True, a...  4.89 us
    pallas_call x1, Pallas kernels, on_device(): pl.pallas_call(functools.partial(down_body, plan, dim, scale), out_shape=...  4.44 us
    ppermute x3, starting transfers between devices, swapped(): return lax.ppermute(value, 'leaf', [(i, i ^ mask) for i in range(subtrees)])  4.36 us
    pallas_call x1, Pallas kernels, on_device(): pl.pallas_call(functools.partial(cross_far_body, plan, dim, scale), out_s...  4.23 us
  transfers between devices with their start and end apart: 7, of which 3 were waited for; matrix products, arithmetic and copies ran while one was open for 1% of the time, Pallas kernels for 42%

profile of v1, /device:TPU:11, one launch (start us, length us, event | category | flops | bytes accessed | tf_op | source)
XLA Modules:
  0.0 58.5 jit_solution(7563000566221337445)
XLA Ops:
  0.0 3.8 %upward.1 = (bf16[32,64,256]{2,1,0:T(8,128)(2,1)}, bf16[4,144,256]{2,1,0:T(8,128)(2,1)}) custom-call(bf16[32,4096]{1,0:T(8,128)(2,1)} %refs_0_.1, bf16[32,4096]{1,0:T(8,128)(2,1)} %refs_1_.1, s32[16,128]{1,0:T(8,128)} %refs_2_.1, s32[15,128]{1,0:T(8,128)} %refs_3_.1, bf16[16,128,256]{2,1,0:T(8,128)(2,1)} %refs_10_.1, bf16[15,128,256]{2,1,0:T(8,128)(2,1)} %refs_9_.1, ...), custom_call_target="tpu_custom_call" | custom-call | flops 1000000000 | bytes 4000000 | tf_op jit(solution)/shard_map/upward/pallas_call | solution.py:545
  3.8 0.7 %collective-permute-start.1 = (bf16[32,64,256]{2,1,0:T(8,128)(2,1)}, bf16[32,64,256]{2,1,0:T(8,128)(2,1)S(1)}, u32[]{:S(2)}, u32[]{:S(2)}) collective-permute-start(bf16[32,64,256]{2,1,0:T(8,128)(2,1)} %get-tuple-element.14.bundle), channel_id=1, source_target_pairs={{0,2},{2,0},{4,6},{6,4},{8,10},{10,8},{12,14},{14,12},{16,18},{18,... | collective-permute-start | bytes 3145736 | tf_op jit(solution)/shard_map/ppermute | solution.py:557
  4.5 4.9 %all-to-all-start = ((bf16[4,144,256]{2,1,0:T(8,128)(2,1)}), bf16[4,144,256]{2,1,0:T(8,128)(2,1)S(1)}, u32[]{:S(2)}, u32[]{:S(2)}) async-start(bf16[4,144,256]{2,1,0:T(8,128)(2,1)} %get-tuple-element.15), calls=%async_computation | async-start | bytes 589824 | tf_op jit(solution)/shard_map/all_to_all | solution.py:559
  9.4 3.6 %collective-permute-start.4 = (bf16[32,64,256]{2,1,0:T(8,128)(2,1)}, bf16[32,64,256]{2,1,0:T(8,128)(2,1)S(1)}, u32[]{:S(2)}, u32[]{:S(2)}) collective-permute-start(bf16[32,64,256]{2,1,0:T(8,128)(2,1)} %get-tuple-element.14.bundle), channel_id=1, source_target_pairs={{2,4},{4,2},{6,8},{8,6},{10,12},{12,10},{14,16},{16,14},{18,20},{2... | collective-permute-start | bytes 3145736 | tf_op jit(solution)/shard_map/ppermute | solution.py:556
  13.1 0.0 copy-done.6
  13.1 0.1 copy.25
  13.2 0.0 copy-done.8
  13.2 0.2 concatenate.3.refs_0_
  13.4 0.3 collective-permute-start
  13.7 0.1 pad_add_fusion.spot
  13.8 2.8 %collective-permute-done.refs_1_ = s32[61,16]{1,0:T(8,128)S(1)} collective-permute-done((s32[61,16]{1,0:T(8,128)S(1)}, s32[61,16]{1,0:T(8,128)S(1)}, u32[]{:S(2)}, u32[]{:S(2)}) %collective-permute-start) | collective-permute-done | bytes 3936 | tf_op jit(solution)/shard_map/ppermute | solution.py:526
  16.6 1.9 %table.1 = s32[16,128]{1,0:T(8,128)S(1)} custom-call(s32[2]{0:T(128)S(1)} %pad_add_fusion.spot, s32[61,16]{1,0:T(8,128)S(1)} %concatenate.3.refs_0_, s32[61,16]{1,0:T(8,128)S(1)} %collective-permute-done.refs_1_), custom_call_target="tpu_custom_call" | custom-call | flops 1000000000 | bytes 4000000 | tf_op jit(solution)/shard_map/table/pallas_call | solution.py:561
  18.5 0.0 all-to-all-done.column
  18.5 0.0 collective-permute-done.1.pair
  18.5 6.7 %near.1 = (f32[8,32,256]{2,1,0:T(8,128)S(1)}, bf16[8,256,48]{2,1,0:T(8,128)(2,1)S(1)}, bf16[4,144,256]{2,1,0:T(8,128)(2,1)S(1)}) custom-call(s32[2]{0:T(128)S(1)} %pad_add_fusion.spot, s32[16,128]{1,0:T(8,128)S(1)} %table.1, bf16[32,64,256]{2,1,0:T(8,128)(2,1)S(1)} %copy-done.5, bf16[32,64,256]{2,1,0:T(8,128)(2,1)S(1)} %collective-permute-done.1.pair, ...), custom_call_target="tpu_custom_call" | custom-call | flops 10000000000 | bytes 4000000 | tf_op jit(solution)/shard_map/near/pallas_call | solution.py:581
  25.2 1.1 %collective-permute-start.3 = (bf16[4,144,256]{2,1,0:T(8,128)(2,1)S(1)}, bf16[4,144,256]{2,1,0:T(8,128)(2,1)S(1)}, u32[]{:S(2)}, u32[]{:S(2)}) collective-permute-start(bf16[4,144,256]{2,1,0:T(8,128)(2,1)S(1)} %get-tuple-element.16.refs_0_), channel_id=1, source_target_pairs={{0,4},{2,6},{4,0},{6,2},{8,12},{10,14},{12,8},{14,10},{16,20},{18,... | collective-permute-start | bytes 884744 | tf_op jit(solution)/shard_map/ppermute | solution.py:593
  26.3 1.6 %collective-permute-start.2 = (bf16[4,144,256]{2,1,0:T(8,128)(2,1)S(1)}, bf16[4,144,256]{2,1,0:T(8,128)(2,1)S(1)}, u32[]{:S(2)}, u32[]{:S(2)}) collective-permute-start(bf16[4,144,256]{2,1,0:T(8,128)(2,1)S(1)} %get-tuple-element.16.refs_0_), channel_id=1, source_target_pairs={{0,2},{2,0},{4,6},{6,4},{8,10},{10,8},{12,14},{14,12},{16,18},{18,... | collective-permute-start | bytes 884744 | tf_op jit(solution)/shard_map/ppermute | solution.py:593
  27.9 7.1 %far.1 = (f32[16,32,128]{2,1,0:T(8,128)S(1)}, bf16[16,128,48]{2,1,0:T(8,128)(2,1)S(1)}) custom-call(s32[2]{0:T(128)S(1)} %pad_add_fusion.spot, s32[16,128]{1,0:T(8,128)S(1)} %table.1, bf16[32,64,256]{2,1,0:T(8,128)(2,1)S(1)} %copy-done.5, bf16[32,64,256]{2,1,0:T(8,128)(2,1)S(1)} %collective-permute-done.1.pair), custom_call_target="tpu_custom_call" | custom-call | flops 10000000000 | bytes 4000000 | tf_op jit(solution)/shard_map/far/pallas_call | solution.py:597
  35.0 5.3 %collective-permute-done.4.cross = bf16[32,64,256]{2,1,0:T(8,128)(2,1)S(1)} collective-permute-done((bf16[32,64,256]{2,1,0:T(8,128)(2,1)}, bf16[32,64,256]{2,1,0:T(8,128)(2,1)S(1)}, u32[]{:S(2)}, u32[]{:S(2)}) %collective-permute-start.4) | collective-permute-done | bytes 1048608 | tf_op jit(solution)/shard_map/ppermute | solution.py:556
  40.3 2.3 %collective-permute-done.3.part.refs_2_ = bf16[4,144,256]{2,1,0:T(8,128)(2,1)S(1)} collective-permute-done((bf16[4,144,256]{2,1,0:T(8,128)(2,1)S(1)}, bf16[4,144,256]{2,1,0:T(8,128)(2,1)S(1)}, u32[]{:S(2)}, u32[]{:S(2)}) %collective-permute-start.3) | collective-permute-done | bytes 294944 | tf_op jit(solution)/shard_map/ppermute | solution.py:593
  42.6 4.2 %crossfar.1 = (f32[16,32,128]{2,1,0:T(8,128)S(1)}, bf16[4,144,256]{2,1,0:T(8,128)(2,1)S(1)}) custom-call(s32[16,128]{1,0:T(8,128)S(1)} %table.1, bf16[32,64,256]{2,1,0:T(8,128)(2,1)S(1)} %collective-permute-done.4.cross, f32[16,32,128]{2,1,0:T(8,128)S(1)} %get-tuple-element.17.far_in, bf16[16,128,48]{2,1,0:T(8,128)(2,1)S(1)} %get-tuple-element.18.goals, ...), custom_call_target="tpu_custom_call" | custom-call | flops 10000000000 | bytes 4000000 | tf_op jit(solution)/shard_map/crossfar/pallas_call | solution.py:608
  46.8 1.6 %collective-permute-start.5 = (bf16[4,144,256]{2,1,0:T(8,128)(2,1)S(1)}, bf16[4,144,256]{2,1,0:T(8,128)(2,1)S(1)}, u32[]{:S(2)}, u32[]{:S(2)}) collective-permute-start(bf16[4,144,256]{2,1,0:T(8,128)(2,1)S(1)} %get-tuple-element.19.part), channel_id=1, source_target_pairs={{0,2},{2,0},{4,6},{6,4},{8,10},{10,8},{12,14},{14,12},{16,18},{18,... | collective-permute-start | bytes 884744 | tf_op jit(solution)/shard_map/ppermute | solution.py:593
  48.5 4.9 %crossnear.1.refs_8_ = f32[8,32,256]{2,1,0:T(8,128)S(1)} custom-call(s32[16,128]{1,0:T(8,128)S(1)} %table.1, bf16[32,64,256]{2,1,0:T(8,128)(2,1)S(1)} %collective-permute-done.4.cross, f32[8,32,256]{2,1,0:T(8,128)S(1)} %get-tuple-element.21.near_in, bf16[8,256,48]{2,1,0:T(8,128)(2,1)S(1)} %get-tuple-element.22.goals, ...), custom_call_target="tpu_custom_call" | custom-call | flops 10000000000 | bytes 4000000 | tf_op jit(solution)/shard_map/crossnear/pallas_call | solution.py:621
  53.4 0.0 copy-start.4
  53.4 0.0 collective-permute-done.2.refs_1_
  53.4 0.0 collective-permute-done.5.refs_3_
  53.4 0.0 copy-done
  53.4 0.0 copy-done.1
  53.4 0.0 copy-done.2
  53.4 0.0 copy-done.3
  53.5 0.6 %copy-done.4 = s32[2,128]{1,0:T(2,128)S(1)} copy-done((s32[2,128]{1,0:T(2,128)S(1)}, s32[2,128]{1,0:T(2,128)}, u32[]{:S(2)}) %copy-start.4) | copy-done | bytes 1048
  54.1 4.4 %down.1 = f32[32,2048]{1,0:T(8,128)} custom-call(s32[2]{0:T(128)S(1)} %pad_add_fusion.spot, s32[16,128]{1,0:T(8,128)S(1)} %table.1, bf16[4,144,256]{2,1,0:T(8,128)(2,1)S(1)} %get-tuple-element.16.refs_0_, bf16[4,144,256]{2,1,0:T(8,128)(2,1)S(1)} %collective-permute-done.2.refs_1_, bf16[4,144,256]{2,1,0:T(8,128)(2,1)S(1)} %collective-permute-done.3.part.refs_2_, ...), custom_call_target="tpu_custom_call" | custom-call | flops 1000000000 | bytes 4000000 | tf_op jit(solution)/shard_map/down/pallas_call | solution.py:632
  (14 shorter events, 0.0 us)
Async XLA Ops:
  3.8 14.7 %collective-permute-start.1 = (bf16[32,64,256]{2,1,0:T(8,128)(2,1)}, bf16[32,64,256]{2,1,0:T(8,128)(2,1)S(1)}, u32[]{:S(2)}, u32[]{:S(2)}) collective-permute-start(bf16[32,64,256]{2,1,0:T(8,128)(2,1)} %get-tuple-element.14.bundle), channel_id=1, source_target_pairs={{0,2},{2,0},{4,6},{6,4},{8,10},{10,8},{12,14},{14,12},{16,18},{18,... | collective-permute-start | bytes 3145736 | tf_op jit(solution)/shard_map/ppermute | solution.py:557
  4.5 8.5 %copy-start.6 = (s32[31,16]{0,1:T(8,128)S(1)}, s32[31,16]{0,1:T(8,128)}, u32[]{:S(2)}) copy-start(s32[31,16]{0,1:T(8,128)} %param.30) | copy-start | bytes 5956
  4.5 14.0 %all-to-all-start = ((bf16[4,144,256]{2,1,0:T(8,128)(2,1)}), bf16[4,144,256]{2,1,0:T(8,128)(2,1)S(1)}, u32[]{:S(2)}, u32[]{:S(2)}) async-start(bf16[4,144,256]{2,1,0:T(8,128)(2,1)} %get-tuple-element.15), calls=%async_computation | async-start | bytes 589824 | tf_op jit(solution)/shard_map/all_to_all | solution.py:559
  9.4 3.7 %copy-start.7 = (s32[16,16]{1,0:T(8,128)S(1)}, s32[16,16]{1,0:T(8,128)}, u32[]{:S(2)}) copy-start(s32[16,16]{1,0:T(8,128)} %param.29) | copy-start | bytes 3076
  9.4 3.7 %copy-start.8 = (s32[8,16]{1,0:T(8,128)S(1)}, s32[8,16]{1,0:T(8,128)}, u32[]{:S(2)}) copy-start(s32[8,16]{1,0:T(8,128)} %param.31) | copy-start | bytes 1540
  9.4 3.7 %copy-start.9 = (s32[4,16]{1,0:T(4,128)S(1)}, s32[4,16]{1,0:T(4,128)}, u32[]{:S(2)}) copy-start(s32[4,16]{1,0:T(4,128)} %param.32) | copy-start | bytes 772
  9.4 3.7 %copy-start.10 = (s32[2,16]{1,0:T(2,128)S(1)}, s32[2,16]{1,0:T(2,128)}, u32[]{:S(2)}) copy-start(s32[2,16]{1,0:T(2,128)} %param.33) | copy-start | bytes 388
  9.4 30.9 %collective-permute-start.4 = (bf16[32,64,256]{2,1,0:T(8,128)(2,1)}, bf16[32,64,256]{2,1,0:T(8,128)(2,1)S(1)}, u32[]{:S(2)}, u32[]{:S(2)}) collective-permute-start(bf16[32,64,256]{2,1,0:T(8,128)(2,1)} %get-tuple-element.14.bundle), channel_id=1, source_target_pairs={{2,4},{4,2},{6,8},{8,6},{10,12},{12,10},{14,16},{16,14},{18,20},{2... | collective-permute-start | bytes 3145736 | tf_op jit(solution)/shard_map/ppermute | solution.py:556
  13.4 3.2 %collective-permute-start = (s32[61,16]{1,0:T(8,128)S(1)}, s32[61,16]{1,0:T(8,128)S(1)}, u32[]{:S(2)}, u32[]{:S(2)}) collective-permute-start(s32[61,16]{1,0:T(8,128)S(1)} %concatenate.3.refs_0_), channel_id=1, source_target_pairs={{0,1},{1,0},{2,3},{3,2},{4,5},{5,4},{6,7},{7,6},{8,9},{9,8},{10,11... | collective-permute-start | bytes 11720 | tf_op jit(solution)/shard_map/ppermute | solution.py:526
  13.8 4.7 %copy-start.5 = (bf16[32,64,256]{2,1,0:T(8,128)(2,1)S(1)}, bf16[32,64,256]{2,1,0:T(8,128)(2,1)}, u32[]{:S(2)}) copy-start(bf16[32,64,256]{2,1,0:T(8,128)(2,1)} %get-tuple-element.14.bundle) | copy-start | bytes 3145732
  25.2 17.4 %collective-permute-start.3 = (bf16[4,144,256]{2,1,0:T(8,128)(2,1)S(1)}, bf16[4,144,256]{2,1,0:T(8,128)(2,1)S(1)}, u32[]{:S(2)}, u32[]{:S(2)}) collective-permute-start(bf16[4,144,256]{2,1,0:T(8,128)(2,1)S(1)} %get-tuple-element.16.refs_0_), channel_id=1, source_target_pairs={{0,4},{2,6},{4,0},{6,2},{8,12},{10,14},{12,8},{14,10},{16,20},{18,... | collective-permute-start | bytes 884744 | tf_op jit(solution)/shard_map/ppermute | solution.py:593
  26.3 27.1 %collective-permute-start.2 = (bf16[4,144,256]{2,1,0:T(8,128)(2,1)S(1)}, bf16[4,144,256]{2,1,0:T(8,128)(2,1)S(1)}, u32[]{:S(2)}, u32[]{:S(2)}) collective-permute-start(bf16[4,144,256]{2,1,0:T(8,128)(2,1)S(1)} %get-tuple-element.16.refs_0_), channel_id=1, source_target_pairs={{0,2},{2,0},{4,6},{6,4},{8,10},{10,8},{12,14},{14,12},{16,18},{18,... | collective-permute-start | bytes 884744 | tf_op jit(solution)/shard_map/ppermute | solution.py:593
  46.8 6.6 %collective-permute-start.5 = (bf16[4,144,256]{2,1,0:T(8,128)(2,1)S(1)}, bf16[4,144,256]{2,1,0:T(8,128)(2,1)S(1)}, u32[]{:S(2)}, u32[]{:S(2)}) collective-permute-start(bf16[4,144,256]{2,1,0:T(8,128)(2,1)S(1)} %get-tuple-element.19.part), channel_id=1, source_target_pairs={{0,2},{2,0},{4,6},{6,4},{8,10},{10,8},{12,14},{14,12},{16,18},{18,... | collective-permute-start | bytes 884744 | tf_op jit(solution)/shard_map/ppermute | solution.py:593
  48.5 5.0 %copy-start = (bf16[16,128,256]{2,1,0:T(8,128)(2,1)S(1)}, bf16[16,128,256]{2,1,0:T(8,128)(2,1)}, u32[]{:S(2)}) copy-start(bf16[16,128,256]{2,1,0:T(8,128)(2,1)} %refs_10_.1) | copy-start | bytes 3145732
  48.5 5.0 %copy-start.1 = (bf16[15,128,256]{2,1,0:T(8,128)(2,1)S(1)}, bf16[15,128,256]{2,1,0:T(8,128)(2,1)}, u32[]{:S(2)}) copy-start(bf16[15,128,256]{2,1,0:T(8,128)(2,1)} %refs_9_.1) | copy-start | bytes 2949124
  48.5 5.0 %copy-start.2 = (s32[8,128]{1,0:T(8,128)S(1)}, s32[8,128]{1,0:T(8,128)}, u32[]{:S(2)}) copy-start(s32[8,128]{1,0:T(8,128)} %refs_4_.3) | copy-start | bytes 12292
  48.5 5.0 %copy-start.3 = (s32[4,128]{1,0:T(4,128)S(1)}, s32[4,128]{1,0:T(4,128)}, u32[]{:S(2)}) copy-start(s32[4,128]{1,0:T(4,128)} %refs_5_.3) | copy-start | bytes 6148
  53.4 0.7 %copy-start.4 = (s32[2,128]{1,0:T(2,128)S(1)}, s32[2,128]{1,0:T(2,128)}, u32[]{:S(2)}) copy-start(s32[2,128]{1,0:T(2,128)} %refs_6_.3) | copy-start | bytes 3076
